TPU v7x, 32 devices: a whole 2x2x4 slice. The times are simulated.
32 devices in a mesh: peer: 4 (over x, core), fsdp: 8 (over z, y).
Axes of the slice: x: 2, y: 2, z: 4, core: 2. Of those that a mesh axis runs over, the one named last changes fastest.
Arguments:
- tokens: bfloat16 [4, 1024, 2048], P('peer', 'fsdp'), may hold values from -6 to 6
- gate_weight: bfloat16 [4, 5632, 2048], P('peer', 'fsdp'), may hold values from -6 to 6
- up_weight: bfloat16 [4, 5632, 2048], P('peer', 'fsdp'), may hold values from -6 to 6
- down_weight: bfloat16 [4, 5632, 2048], P('peer', 'fsdp'), may hold values from -6 to 6
- cotangent: bfloat16 [4, 1024, 2048], P('peer', 'fsdp'), may hold values from -6 to 6
Outputs:
- new_gate: bfloat16 [4, 5632, 2048], P('peer', 'fsdp')
- new_up: bfloat16 [4, 5632, 2048], P('peer', 'fsdp')
All inputs are finite; a program needn't handle non-finite values.
Results may differ from a plain program's by a relative error of at most 0.0054.
Values may be sent and summed in bfloat16 or wider, within the bound.
A program may use at most 128 MiB of HBM per device.

v0:
```python
import jax
import jax.numpy as jnp
from jax import lax
from jax.sharding import PartitionSpec as P

D = 2048
FF = 5632
HOP = 2


rate_value = 1.0


def passed_along(shard, axis, by):
    peers = lax.axis_size(axis)
    return lax.ppermute(shard, axis, [(i, (i + by) % peers) for i in range(peers)])


def across_features(left, right):
    return lax.dot_general(
        left, right, (((1,), (1,)), ((), ())), preferred_element_type=jnp.float32
    )


def across_rows(left, right):
    return lax.dot_general(
        left, right, (((0,), (0,)), ((), ())), preferred_element_type=jnp.float32
    )


def project_rows(piece, gate_local, upper_local):
    factor = D ** (-0.5)
    return (
        across_features(piece, gate_local) * factor,
        across_features(piece, upper_local) * factor,
    )


def weight_terms(cot_rows, token_block, gate_rows, upper_rows, down_local):
    dhidden = across_features(cot_rows, down_local) * FF ** (-0.5)
    sigma = jax.nn.sigmoid(gate_rows)
    dgate = (dhidden * upper_rows * sigma * (1.0 + gate_rows * (1.0 - sigma))).astype(jnp.bfloat16)
    dupper = (dhidden * gate_rows * sigma).astype(jnp.bfloat16)
    return (across_rows(dgate, token_block), across_rows(dupper, token_block))


def stepped(local, grad):
    return (local.astype(jnp.float32) - rate_value * (grad * D ** (-0.5))).astype(jnp.bfloat16)


def averaged(mine, theirs):
    return ((mine.astype(jnp.float32) + theirs.astype(jnp.float32)) * 0.5).astype(jnp.bfloat16)


def body(tokens, gate_weight, up_weight, down_weight, cotangent):
    own_tokens = tokens[0]
    own_cotangent = cotangent[0]
    gate_local = gate_weight[0]
    upper_local = up_weight[0]
    down_local = down_weight[0]
    piece = lax.all_gather(own_tokens, "fsdp", axis=0, tiled=True)
    gate_part, upper_part = project_rows(piece, gate_local, upper_local)
    first, second = weight_terms(
        lax.all_gather(own_cotangent, "fsdp", axis=0, tiled=True),
        piece,
        gate_part,
        upper_part,
        down_local,
    )
    stepped_gate = stepped(gate_local, first)
    stepped_upper = stepped(upper_local, second)
    partner_gate, partner_upper = passed_along((stepped_gate, stepped_upper), "peer", HOP)
    new_gate = averaged(stepped_gate, partner_gate)
    new_upper = averaged(stepped_upper, partner_upper)
    return (new_gate[None], new_upper[None])


def solution(mesh):
    return jax.shard_map(
        body,
        mesh=mesh,
        in_specs=(
            P("peer", "fsdp", None),
            P("peer", "fsdp", None),
            P("peer", "fsdp", None),
            P("peer", "fsdp", None),
            P("peer", "fsdp", None),
        ),
        out_specs=(P("peer", "fsdp", None), P("peer", "fsdp", None)),
        check_vma=False,
    )
```

profile of v0, /device:TPU:0, one launch (start us, length us, event | category | flops | bytes accessed | tf_op | source)
XLA Modules:
  0.0 308.3 jit_solution(17562290344428333540)
XLA Ops:
  7.2 0.0 copy-start
  7.2 0.0 all-gather.5.cloned.1.call-start
  7.2 0.7 all-gather.5.cloned.1.call-update
  7.9 0.0 all-gather.7.cloned.1.call-start
  8.0 0.7 all-gather.7.cloned.1.call-update
  8.7 77.6 %all-gather.5.cloned.1.call-done = bf16[1,1024,2048]{2,1,0:T(8,128)(2,1)} async-done(((bf16[1,128,2048]{2,1,0:T(8,128)(2,1)}), bf16[1,1024,2048]{2,1,0:T(8,128)(2,1)}) %all-gather.5.cloned.1.call-update) | async-done | bytes 4194320 | tf_op jit(solution)/shard_map/all_gather | solution.py:64
  86.3 0.0 copy-done
  86.3 6.9 %fusion.8 = f32[1024,704]{0,1:T(8,128)} fusion(bf16[1,1024,2048]{2,1,0:T(8,128)(2,1)} %all-gather.5.cloned.1.call-done, bf16[1,704,2048]{2,1,0:T(8,128)(2,1)S(1)} %copy-done), kind=kOutput, calls=%fused_computation.12 | convolution fusion | flops 2952790016 | bytes 9961472 | tf_op jit(solution)/shard_map/dot_general | solution.py:20
  93.2 66.9 %all-gather.7.cloned.1.call-done = bf16[1,1024,2048]{2,1,0:T(8,128)(2,1)} async-done(((bf16[1,128,2048]{2,1,0:T(8,128)(2,1)}), bf16[1,1024,2048]{2,1,0:T(8,128)(2,1)}) %all-gather.7.cloned.1.call-update) | async-done | bytes 4194320 | tf_op jit(solution)/shard_map/all_gather | solution.py:61
  160.1 0.0 copy-start.1
  160.1 0.0 copy-start.3
  160.1 0.0 copy-start.4
  160.1 6.0 %fusion.4 = f32[1024,704]{0,1:T(8,128)S(1)} fusion(bf16[1,1024,2048]{2,1,0:T(8,128)(2,1)} %all-gather.7.cloned.1.call-done, bf16[1,704,2048]{2,1,0:T(8,128)(2,1)} %param.6), kind=kOutput, calls=%fused_computation.8 | convolution fusion | flops 2952790016 | bytes 9961472 | tf_op jit(solution)/shard_map/dot_general | solution.py:20
  166.1 0.0 copy-done.1
  166.1 0.0 copy-done.3
  166.1 0.0 copy-done.4
  166.1 0.0 copy-start.2
  166.1 4.1 %multiply_convert_fusion.3 = bf16[1024,704]{0,1:T(8,128)(2,1)S(1)} fusion(f32[1024,704]{0,1:T(8,128)S(1)} %fusion.4, f32[1024,704]{0,1:T(8,128)S(1)} %copy-done.4, bf16[1,704,2048]{2,1,0:T(8,128)(2,1)S(1)} %copy-done.3, bf16[1,1024,2048]{2,1,0:T(8,128)(2,1)S(1)} %copy-done.1), kind=kOutput, calls=%fused_computation.20 | convolution fusion | flops 2962161664 | bytes 14286848 | tf_op jit(solution)/shard_map/dot_general | solution.py:20
  170.3 0.0 copy-done.2
  170.3 3.4 %subtract_convert_fusion.1 = bf16[704,2048]{1,0:T(8,128)(2,1)S(1)} fusion(bf16[1024,704]{0,1:T(8,128)(2,1)S(1)} %multiply_convert_fusion.3, bf16[1,1024,2048]{2,1,0:T(8,128)(2,1)S(1)} %copy-done.1, bf16[1,704,2048]{2,1,0:T(8,128)(2,1)S(1)} %copy-done.2), kind=kOutput, calls=%fused_computation.3 | convolution fusion | flops 2958557184 | bytes 11403264 | tf_op jit(solution)/shard_map/dot_general | solution.py:26
  173.7 1.5 collective-permute-start
  175.2 3.7 %subtract_convert_fusion = bf16[704,2048]{1,0:T(8,128)(2,1)S(1)} fusion(bf16[1,1024,2048]{2,1,0:T(8,128)(2,1)S(1)} %copy-done.1, bf16[1,704,2048]{2,1,0:T(8,128)(2,1)S(1)} %copy-done.3, f32[1024,704]{0,1:T(8,128)S(1)} %fusion.4, f32[1024,704]{0,1:T(8,128)S(1)} %copy-done.4), kind=kOutput, calls=%fused_computation.1 | convolution fusion | flops 2964324352 | bytes 15728640 | tf_op jit(solution)/shard_map/dot_general | solution.py:26
  178.9 0.6 collective-permute-start.1
  179.6 59.6 %collective-permute-done = bf16[704,2048]{1,0:T(8,128)(2,1)S(1)} collective-permute-done((bf16[704,2048]{1,0:T(8,128)(2,1)S(1)}, bf16[704,2048]{1,0:T(8,128)(2,1)S(1)}, u32[]{:S(2)}, u32[]{:S(2)}) %collective-permute-start) | collective-permute-done | bytes 2883616 | tf_op jit(solution)/shard_map/ppermute | solution.py:16
  239.2 2.9 fusion.14
  242.1 56.5 %collective-permute-done.1 = bf16[704,2048]{1,0:T(8,128)(2,1)S(1)} collective-permute-done((bf16[704,2048]{1,0:T(8,128)(2,1)S(1)}, bf16[704,2048]{1,0:T(8,128)(2,1)S(1)}, u32[]{:S(2)}, u32[]{:S(2)}) %collective-permute-start.1) | collective-permute-done | bytes 2883616 | tf_op jit(solution)/shard_map/ppermute | solution.py:16
  298.6 2.9 fusion.15
Async XLA Ops:
  7.2 79.1 %copy-start = (bf16[1,704,2048]{2,1,0:T(8,128)(2,1)S(1)}, bf16[1,704,2048]{2,1,0:T(8,128)(2,1)}, u32[]{:S(2)}) copy-start(bf16[1,704,2048]{2,1,0:T(8,128)(2,1)} %param.8) | copy-start | bytes 8650756
  7.2 79.1 %all-gather.5.cloned.1.call-start = ((), (), s32[]{:S(2)}) async-start(), calls=%async_computation | async-start | bytes 4718592 | tf_op jit(solution)/shard_map/all_gather | solution.py:64
  7.9 152.2 %all-gather.7.cloned.1.call-start = ((), (), s32[]{:S(2)}) async-start(), calls=%async_computation.1 | async-start | bytes 4718592 | tf_op jit(solution)/shard_map/all_gather | solution.py:61
  160.1 6.0 %copy-start.1 = (bf16[1,1024,2048]{2,1,0:T(8,128)(2,1)S(1)}, bf16[1,1024,2048]{2,1,0:T(8,128)(2,1)}, u32[]{:S(2)}) copy-start(bf16[1,1024,2048]{2,1,0:T(8,128)(2,1)} %all-gather.7.cloned.1.call-done) | copy-start | bytes 12582916
  160.1 6.0 %copy-start.3 = (bf16[1,704,2048]{2,1,0:T(8,128)(2,1)S(1)}, bf16[1,704,2048]{2,1,0:T(8,128)(2,1)}, u32[]{:S(2)}) copy-start(bf16[1,704,2048]{2,1,0:T(8,128)(2,1)} %param.7) | copy-start | bytes 8650756
  160.1 6.0 %copy-start.4 = (f32[1024,704]{0,1:T(8,128)S(1)}, f32[1024,704]{0,1:T(8,128)}, u32[]{:S(2)}) copy-start(f32[1024,704]{0,1:T(8,128)} %fusion.8) | copy-start | bytes 8650756
  166.1 4.1 %copy-start.2 = (bf16[1,704,2048]{2,1,0:T(8,128)(2,1)S(1)}, bf16[1,704,2048]{2,1,0:T(8,128)(2,1)}, u32[]{:S(2)}) copy-start(bf16[1,704,2048]{2,1,0:T(8,128)(2,1)} %param.6) | copy-start | bytes 8650756
  173.7 65.5 %collective-permute-start = (bf16[704,2048]{1,0:T(8,128)(2,1)S(1)}, bf16[704,2048]{1,0:T(8,128)(2,1)S(1)}, u32[]{:S(2)}, u32[]{:S(2)}) collective-permute-start(bf16[704,2048]{1,0:T(8,128)(2,1)S(1)} %subtract_convert_fusion.1), channel_id=1, source_target_pairs={{0,16},{8,24},{16,0},{24,8},{1,17},{9,25},{17,1},{25,9},{2,18},{10... | collective-permute-start | bytes 8650760 | tf_op jit(solution)/shard_map/ppermute | solution.py:16
  178.9 119.7 %collective-permute-start.1 = (bf16[704,2048]{1,0:T(8,128)(2,1)S(1)}, bf16[704,2048]{1,0:T(8,128)(2,1)S(1)}, u32[]{:S(2)}, u32[]{:S(2)}) collective-permute-start(bf16[704,2048]{1,0:T(8,128)(2,1)S(1)} %subtract_convert_fusion), channel_id=1, source_target_pairs={{0,16},{8,24},{16,0},{24,8},{1,17},{9,25},{17,1},{25,9},{2,18},{10... | collective-permute-start | bytes 8650760 | tf_op jit(solution)/shard_map/ppermute | solution.py:16
Sparse Core Ops, SparseCore 0:
  10.1 76.0 all-gather.4
  88.4 71.6 all-gather.6
where the time goes:
time: 308 us
  waiting for transfers between devices  262 us (85%)
  matrix products  24.1 us (8%)
  between operations  14.1 us (5%)
  other arithmetic  5.76 us (2%)
    ppermute x2, waiting for transfers between devices, passed_along(): lax.ppermute(shard, axis, [(i, (i + by) % peers) for i in range(peers)])  116 us
    all_gather x1, waiting for transfers between devices, body(): lax.all_gather(own_cotangent, 'fsdp', axis=0, tiled=True)  77.6 us
    all_gather x1, waiting for transfers between devices, body(): piece = lax.all_gather(own_tokens, 'fsdp', axis=0, tiled=True)  66.9 us
    dot_general x3, matrix products, across_features(): lax.dot_general(left, right, (((1,), (1,)), ((), ())), preferred_element_...  17 us
    dot_general x2, matrix products, across_rows(): lax.dot_general(left, right, (((0,), (0,)), ((), ())), preferred_element_...  7.11 us
  transfers between devices with their start and end apart: 4, of which 4 were waited for; matrix products, arithmetic and copies ran while one was open for 4% of the time, Pallas kernels for 0%

commit v1 on v0

v1 whole, which is shorter than its diff:
```python
import functools

import jax
import jax.numpy as jnp
from jax import lax
from jax.experimental import pallas as pl
from jax.experimental.pallas import tpu as pltpu
from jax.sharding import PartitionSpec as P

HOP = 2
CHUNKS = 11
RATE = 1.0
MESH = pl.DeviceIdType.MESH


def nt(left, right):
    return lax.dot_general(
        left, right, (((1,), (1,)), ((), ())), preferred_element_type=jnp.float32
    )


def kernel(
    fsdp,
    peers,
    tok_in,
    gate_in,
    up_in,
    down_in,
    cot_in,
    gate_out,
    up_out,
    tok,
    cot,
    wg,
    wu,
    wd,
    dgate,
    dup,
    own,
    landed,
    load_sem,
    send_sem,
    recv_sem,
    peer_send,
    peer_recv,
    out_sem,
):
    part, width = tok_in.shape[1], tok_in.shape[2]
    rows = gate_in.shape[1]
    chunk = rows // CHUNKS
    in_scale = width ** (-0.5)
    hidden_scale = (rows * fsdp) ** (-0.5)
    deep = fsdp // 2

    me = lax.axis_index("fsdp")
    peer = lax.axis_index("peer")
    z, y = me // 2, me % 2
    across = z * 2 + 1 - y
    to_peer = lax.rem(peer + HOP, peers)
    from_peer = lax.rem(peer + peers - HOP, peers)
    has_prev, has_next = z > 0, z < deep - 1

    ins = (tok_in, cot_in)
    bufs = (tok, cot)

    loads = [
        pltpu.make_async_copy(source.at[0], target, load_sem.at[k])
        for k, (source, target) in enumerate(((gate_in, wg), (up_in, wu), (down_in, wd)))
    ]

    def span(origin):
        return pl.ds(pl.multiple_of(origin * part, part), part)

    loads += [
        pltpu.make_async_copy(ins[a].at[0], bufs[a].at[span(me), :], load_sem.at[3 + a])
        for a in range(2)
    ]
    for load in reversed(loads):
        load.start()

    barrier = pltpu.get_barrier_semaphore()

    def greet(target):
        pl.semaphore_signal(barrier, inc=1, device_id=target, device_id_type=MESH)

    greet({"fsdp": across})
    greet({"peer": to_peer})
    greet({"peer": from_peer})

    @pl.when(has_prev)
    def _():
        greet({"fsdp": me - 2})

    @pl.when(has_next)
    def _():
        greet({"fsdp": me + 2})

    pl.semaphore_wait(barrier, 3 + has_prev.astype(jnp.int32) + has_next.astype(jnp.int32))

    def hop(a, origin, way, first=False):
        target = (me + 2, me - 2, across)[way]
        here = bufs[a].at[span(origin), :]
        return pltpu.make_async_remote_copy(
            src_ref=ins[a].at[0] if first else here,
            dst_ref=here,
            send_sem=send_sem.at[a, origin, way],
            recv_sem=recv_sem.at[a, origin],
            device_id={"fsdp": target},
            device_id_type=MESH,
        )

    def arrive(a, origin):
        hop(a, origin, 2).wait_recv()

    for a in range(2):
        @pl.when(has_next)
        def _():
            hop(a, me, 0, True).start()

        @pl.when(has_prev)
        def _():
            hop(a, me, 1, True).start()

        hop(a, me, 2, True).start()

    def forward(origin):
        lanes = span(origin)
        half = rows // 2

        def some(i, carry):
            at = pl.ds(pl.multiple_of(i * half, half), half)
            gate = nt(wg[at, :], tok[lanes, :]) * in_scale
            upper = nt(wu[at, :], tok[lanes, :]) * in_scale
            dhidden = nt(wd[at, :], cot[lanes, :]) * hidden_scale
            sigma = jax.nn.sigmoid(gate)
            dgate[at, lanes] = (
                dhidden * upper * sigma * (1.0 + gate * (1.0 - sigma))
            ).astype(jnp.bfloat16)
            dup[at, lanes] = (dhidden * gate * sigma).astype(jnp.bfloat16)
            return carry

        lax.fori_loop(0, 2, some, 0)

    for load in loads:
        load.wait()
    forward(me)

    for step in range(1, deep + 1):
        left, right = me - 2 * step, me + 2 * step
        has_left, has_right = z - step >= 0, z + step < deep
        near_left, near_right = across - 2 * (step - 1), across + 2 * (step - 1)
        has_near_left, has_near_right = z - step + 1 >= 0, z + step - 1 < deep
        for a in range(2):
            if step < deep:
                @pl.when(has_left)
                def _():
                    arrive(a, left)

                    @pl.when(has_next)
                    def _():
                        hop(a, left, 0).start()

                    hop(a, left, 2).start()

                @pl.when(has_right)
                def _():
                    arrive(a, right)

                    @pl.when(has_prev)
                    def _():
                        hop(a, right, 1).start()

                    hop(a, right, 2).start()

        if step < deep:
            @pl.when(has_left)
            def _():
                forward(left)

            @pl.when(has_right)
            def _():
                forward(right)

        @pl.when(has_near_left)
        def _():
            for a in range(2):
                arrive(a, near_left)
            forward(near_left)

        if step > 1:
            @pl.when(has_near_right)
            def _():
                for a in range(2):
                    arrive(a, near_right)
                forward(near_right)

    def rows_of(c):
        return pl.ds(pl.multiple_of(c * chunk, chunk), chunk)

    def exchange(c):
        return pltpu.make_async_remote_copy(
            src_ref=own.at[c],
            dst_ref=landed.at[c],
            send_sem=peer_send.at[c],
            recv_sem=peer_recv.at[c],
            device_id={"peer": to_peer},
            device_id_type=MESH,
        )

    def update(c, carry):
        at = rows_of(c)
        grad = jnp.dot(
            jnp.concatenate([dgate[at, :], dup[at, :]], axis=0),
            tok[...],
            preferred_element_type=jnp.float32,
        ) * in_scale
        weight = jnp.concatenate([wg[at, :], wu[at, :]], axis=0).astype(jnp.float32)
        own[c] = (weight - RATE * grad).astype(jnp.bfloat16)
        exchange(c).start()
        return carry

    lax.fori_loop(0, CHUNKS, update, 0)

    def results(c):
        at = rows_of(c)
        return (
            pltpu.make_async_copy(
                landed.at[c, pl.ds(0, chunk), :], gate_out.at[0, at, :], out_sem.at[0, c]
            ),
            pltpu.make_async_copy(
                landed.at[c, pl.ds(chunk, chunk), :], up_out.at[0, at, :], out_sem.at[1, c]
            ),
        )

    def average(c, carry):
        exchange(c).wait_recv()
        landed[c] = (
            (own[c].astype(jnp.float32) + landed[c].astype(jnp.float32)) * 0.5
        ).astype(jnp.bfloat16)
        for copy in results(c):
            copy.start()
        return carry

    lax.fori_loop(0, CHUNKS, average, 0)

    def finish(c, carry):
        exchange(c).wait_send()
        for copy in results(c):
            copy.wait()
        return carry

    lax.fori_loop(0, CHUNKS, finish, 0)

    for a in range(2):
        for step in range(deep):
            left, right = me - 2 * step, me + 2 * step

            @pl.when(z - step >= 0)
            def _():
                @pl.when(has_next)
                def _():
                    hop(a, left, 0).wait_send()

                hop(a, left, 2).wait_send()

            @pl.when(z + step < deep)
            def _():
                @pl.when(has_prev)
                def _():
                    hop(a, right, 1).wait_send()

                if step > 0:
                    hop(a, right, 2).wait_send()


def solution(mesh):
    fsdp, peers = mesh.shape["fsdp"], mesh.shape["peer"]

    def body(tokens, gate_weight, up_weight, down_weight, cotangent):
        _, part, width = tokens.shape
        rows = gate_weight.shape[1]
        every = part * fsdp
        bf16 = jnp.bfloat16
        result = jax.ShapeDtypeStruct((1, rows, width), bf16)
        flops = 10 * every * rows * width
        return pl.pallas_call(
            functools.partial(kernel, fsdp, peers),
            out_shape=(result, result),
            in_specs=[pl.BlockSpec(memory_space=pl.ANY)] * 5,
            out_specs=(pl.BlockSpec(memory_space=pl.ANY),) * 2,
            scratch_shapes=[
                pltpu.VMEM((every, width), bf16),
                pltpu.VMEM((every, width), bf16),
                pltpu.VMEM((rows, width), bf16),
                pltpu.VMEM((rows, width), bf16),
                pltpu.VMEM((rows, width), bf16),
                pltpu.VMEM((rows, every), bf16),
                pltpu.VMEM((rows, every), bf16),
                pltpu.VMEM((CHUNKS, 2 * rows // CHUNKS, width), bf16),
                pltpu.VMEM((CHUNKS, 2 * rows // CHUNKS, width), bf16),
                pltpu.SemaphoreType.DMA((5,)),
                pltpu.SemaphoreType.DMA((2, fsdp, 3)),
                pltpu.SemaphoreType.DMA((2, fsdp)),
                pltpu.SemaphoreType.DMA((CHUNKS,)),
                pltpu.SemaphoreType.DMA((CHUNKS,)),
                pltpu.SemaphoreType.DMA((2, CHUNKS)),
            ],
            compiler_params=pltpu.CompilerParams(
                collective_id=0, has_side_effects=True, vmem_limit_bytes=56 * 2**20
            ),
            cost_estimate=pl.CostEstimate(
                flops=flops, bytes_accessed=10 * rows * width, transcendentals=every * rows
            ),
        )(tokens, gate_weight, up_weight, down_weight, cotangent)

    spec = P("peer", "fsdp", None)
    return jax.shard_map(
        body, mesh=mesh, in_specs=(spec,) * 5, out_specs=(spec, spec), check_vma=False
    )
```

time: 308 us -> 232 us (0.75)
  waiting for transfers between devices: 262 us -> 0 us
  Pallas kernels: 0 us -> 225 us
  matrix products: 24.1 us -> 0 us
  between operations: 14.1 us -> 0.65 us
  other arithmetic: 5.76 us -> 0 us
  local copies, waits for them, and re-layouts: 0.03 us -> 5.5 us
    pallas_call x0 -> x1, Pallas kernels: none -> 225 us  [body(): pl.pallas_call(functools.partial(kernel, fsdp, peers), out_shape=(result,...]
    all_gather x2 -> x0, waiting for transfers between devices: 144 us -> none  [the longest x1 77.6 us: body(): lax.all_gather(own_cotangent, 'fsdp', axis=0, tiled=True)]
    ppermute x2 -> x0, waiting for transfers between devices: 116 us -> none  [passed_along(): lax.ppermute(shard, axis, [(i, (i + by) % peers) for i in range(peers)])]
    dot_general x5 -> x0, matrix products: 24.1 us -> none  [the longest x3 17 us: across_features(): lax.dot_general(left, right, (((1,), (1,)), ((), ())), preferred_element_...]
    broadcast_in_dim x2 -> x0, other arithmetic: 5.76 us -> none  [body(): return (new_gate[None], new_upper[None])]
    unnamed x10 -> x4, local copies, waits for them, and re-layouts: 0.03 us -> 5.5 us
  transfers between devices with their start and end apart: 4 -> 0, of which waited for: 4 -> 0; matrix products, arithmetic and copies ran while one was open for 4% -> 0% of each run, Pallas kernels for 0% -> 0%
where the time goes in v1:
time: 232 us; the launch traced here: 231 us
  Pallas kernels  225 us (97%)
  local copies, waits for them, and re-layouts  5.5 us (2%)
    pallas_call x1, Pallas kernels, body(): pl.pallas_call(functools.partial(kernel, fsdp, peers), out_shape=(result,...  225 us
    unnamed x4, local copies, waits for them, and re-layouts  5.5 us

profile of v1, /device:TPU:0, one launch (start us, length us, event | category | flops | bytes accessed | tf_op | source)
XLA Modules:
  0.0 231.5 jit_solution(14904802448451214033)
XLA Ops:
  0.6 225.4 %shard_map.68 = (bf16[1,704,2048]{2,1,0:T(8,128)(2,1)}, bf16[1,704,2048]{2,1,0:T(8,128)(2,1)}) custom-call(bf16[1,128,2048]{2,1,0:T(8,128)(2,1)} %tok_in.1, bf16[1,704,2048]{2,1,0:T(8,128)(2,1)} %gate_in.1, bf16[1,704,2048]{2,1,0:T(8,128)(2,1)} %up_in.1, bf16[1,704,2048]{2,1,0:T(8,128)(2,1)} %down_in.1, bf16[1,128,2048]{2,1,0:T(8,128)(2,1)} %cot_in.1), custom_call_target="tpu_custom_call" | custom-call | flops 14763950080 | bytes 14417920 | tf_op jit(solution)/shard_map/pallas_call | solution.py:286
  226.0 0.0 copy-start
  226.0 3.9 %copy.9 = bf16[1,704,2048]{2,1,0:T(8,128)(2,1)} copy(bf16[1,704,2048]{2,1,0:T(8,128)(2,1)} %get-tuple-element.4) | data formatting | bytes 5767168
  229.9 0.0 copy-done
  229.9 1.6 copy.10
Async XLA Ops:
  226.0 3.9 %copy-start = (bf16[1,704,2048]{2,1,0:T(8,128)(2,1)S(1)}, bf16[1,704,2048]{2,1,0:T(8,128)(2,1)}, u32[]{:S(2)}) copy-start(bf16[1,704,2048]{2,1,0:T(8,128)(2,1)} %get-tuple-element.5) | copy-start | bytes 8650756

commit v2 on v1

v2 whole, which is shorter than its diff:
```python
import functools

import jax
import jax.numpy as jnp
from jax import lax
from jax.experimental import pallas as pl
from jax.experimental.pallas import tpu as pltpu
from jax.sharding import PartitionSpec as P

HOP = 2
CHUNKS = 11
EARLY = 5
LATE = CHUNKS - EARLY
RATE = 1.0
MESH = pl.DeviceIdType.MESH


def nt(left, right):
    return lax.dot_general(
        left, right, (((1,), (1,)), ((), ())), preferred_element_type=jnp.float32
    )


def kernel(
    fsdp,
    peers,
    tok_in,
    gate_in,
    up_in,
    down_in,
    cot_in,
    gate_out,
    up_out,
    tok,
    cot,
    wg,
    wu,
    wd,
    tok_theirs,
    dhid,
    dhid_theirs,
    weight_theirs,
    own,
    landed,
    load_sem,
    send_sem,
    recv_sem,
    peer_send,
    peer_recv,
    raw_send,
    raw_recv,
    dhid_send,
    dhid_recv,
    out_sem,
):
    part, width = tok_in.shape[1], tok_in.shape[2]
    rows = gate_in.shape[1]
    chunk = rows // CHUNKS
    in_scale = width ** (-0.5)
    hidden_scale = (rows * fsdp) ** (-0.5)
    deep = fsdp // 2

    me = lax.axis_index("fsdp")
    peer = lax.axis_index("peer")
    z, y = me // 2, me % 2
    across = z * 2 + 1 - y
    to_peer = lax.rem(peer + HOP, peers)
    from_peer = lax.rem(peer + peers - HOP, peers)
    has_prev, has_next = z > 0, z < deep - 1

    ins = (tok_in, cot_in)
    bufs = (tok, cot, tok_theirs)
    early_rows = pl.ds(LATE * chunk, EARLY * chunk)

    loads = [
        pltpu.make_async_copy(source.at[0], target, load_sem.at[k])
        for k, (source, target) in enumerate(((gate_in, wg), (up_in, wu), (down_in, wd)))
    ]

    def span(origin):
        return pl.ds(pl.multiple_of(origin * part, part), part)

    loads += [
        pltpu.make_async_copy(ins[a].at[0], bufs[a].at[span(me), :], load_sem.at[3 + a])
        for a in range(2)
    ]
    for load in reversed(loads):
        load.start()

    barrier = pltpu.get_barrier_semaphore()

    def greet(target):
        pl.semaphore_signal(barrier, inc=1, device_id=target, device_id_type=MESH)

    greet({"fsdp": across})
    greet({"peer": to_peer})
    greet({"peer": from_peer})

    @pl.when(has_prev)
    def _():
        greet({"fsdp": me - 2})

    @pl.when(has_next)
    def _():
        greet({"fsdp": me + 2})

    pl.semaphore_wait(barrier, 3 + has_prev.astype(jnp.int32) + has_next.astype(jnp.int32))

    def hop(a, origin, way, first=False):
        target = (me + 2, me - 2, across)[way]
        here = bufs[a].at[span(origin), :]
        return pltpu.make_async_remote_copy(
            src_ref=ins[a].at[0] if first else here,
            dst_ref=here,
            send_sem=send_sem.at[a, origin, way],
            recv_sem=recv_sem.at[a, origin],
            device_id={"fsdp": target},
            device_id_type=MESH,
        )

    def arrive(a, origin):
        hop(a, origin, 2).wait_recv()

    def first_hops(a, first):
        @pl.when(has_next)
        def _():
            hop(a, me, 0, first).start()

        @pl.when(has_prev)
        def _():
            hop(a, me, 1, first).start()

        hop(a, me, 2, first).start()

    for a in range(2):
        first_hops(a, True)

    def to_partner(source, target, sent, received):
        return pltpu.make_async_remote_copy(
            src_ref=source,
            dst_ref=target,
            send_sem=sent,
            recv_sem=received,
            device_id={"peer": to_peer},
            device_id_type=MESH,
        )

    raw = [
        to_partner(source, target, raw_send.at[k], raw_recv.at[k])
        for k, (source, target) in enumerate(
            (
                (tok_in.at[0], tok_theirs.at[span(me), :]),
                (gate_in.at[0, early_rows, :], weight_theirs.at[0]),
                (up_in.at[0, early_rows, :], weight_theirs.at[1]),
            )
        )
    ]
    for copy in raw:
        copy.start()

    def pass_dhid(origin):
        return to_partner(
            dhid.at[:, early_rows, span(origin)],
            dhid_theirs.at[:, :, span(origin)],
            dhid_send.at[origin],
            dhid_recv.at[origin],
        )

    def forward(origin):
        lanes = span(origin)
        half = rows // 2

        def some(i, carry):
            at = pl.ds(pl.multiple_of(i * half, half), half)
            gate = nt(wg[at, :], tok[lanes, :]) * in_scale
            upper = nt(wu[at, :], tok[lanes, :]) * in_scale
            dhidden = nt(wd[at, :], cot[lanes, :]) * hidden_scale
            sigma = jax.nn.sigmoid(gate)
            dhid[0, at, lanes] = (
                dhidden * upper * sigma * (1.0 + gate * (1.0 - sigma))
            ).astype(jnp.bfloat16)
            dhid[1, at, lanes] = (dhidden * gate * sigma).astype(jnp.bfloat16)
            return carry

        lax.fori_loop(0, 2, some, 0)
        pass_dhid(origin).start()

    for load in loads:
        load.wait()
    forward(me)

    def relay(step, arrays):
        left, right = me - 2 * step, me + 2 * step
        for a in arrays:
            @pl.when(z - step >= 0)
            def _():
                arrive(a, left)

                @pl.when(has_next)
                def _():
                    hop(a, left, 0).start()

                hop(a, left, 2).start()

            @pl.when(z + step < deep)
            def _():
                arrive(a, right)

                @pl.when(has_prev)
                def _():
                    hop(a, right, 1).start()

                hop(a, right, 2).start()

    def gather(step, arrays, use):
        left, right = me - 2 * step, me + 2 * step
        near_left, near_right = across - 2 * (step - 1), across + 2 * (step - 1)
        if step < deep:
            relay(step, arrays)
            if use is forward:
                if step == deep - 1:
                    raw[0].wait_recv()
                    first_hops(2, False)

                @pl.when(z - step >= 0)
                def _():
                    forward(left)

                @pl.when(z + step < deep)
                def _():
                    forward(right)

        @pl.when(z - step + 1 >= 0)
        def _():
            for a in arrays:
                arrive(a, near_left)
            use(near_left)

        if step > 1:
            @pl.when(z + step - 1 < deep)
            def _():
                for a in arrays:
                    arrive(a, near_right)
                use(near_right)

    for step in range(1, deep + 1):
        gather(step, (0, 1), forward)

    def rows_of(c):
        return pl.ds(pl.multiple_of(c * chunk, chunk), chunk)

    def exchange(c):
        return to_partner(own.at[c], landed.at[c], peer_send.at[c], peer_recv.at[c])

    def both(ref, at):
        return jnp.concatenate([ref[0, at, :], ref[1, at, :]], axis=0)

    def stepped(weight, terms, tokens):
        grad = jnp.dot(terms, tokens, preferred_element_type=jnp.float32) * in_scale
        return (weight.astype(jnp.float32) - RATE * grad).astype(jnp.bfloat16)

    def averaged(mine, theirs):
        return (
            (mine.astype(jnp.float32) + theirs.astype(jnp.float32)) * 0.5
        ).astype(jnp.bfloat16)

    def step_own(c):
        at = rows_of(c)
        weight = jnp.concatenate([wg[at, :], wu[at, :]], axis=0)
        own[c] = stepped(weight, both(dhid, at), tok[...])

    def late(c, carry):
        step_own(c)
        exchange(c).start()
        return carry

    def early(c, carry):
        step_own(c)
        return carry

    def unused(origin):
        pass

    begin = 0
    for step in range(1, deep + 1):
        end = -(-LATE * step // deep)
        lax.fori_loop(begin, end, late, 0)
        begin = end
        gather(step, (2,), unused)
    lax.fori_loop(LATE, CHUNKS, early, 0)

    def results(c, ref, at):
        return (
            pltpu.make_async_copy(
                ref.at[c, pl.ds(0, chunk), :], gate_out.at[0, at, :], out_sem.at[0, c]
            ),
            pltpu.make_async_copy(
                ref.at[c, pl.ds(chunk, chunk), :], up_out.at[0, at, :], out_sem.at[1, c]
            ),
        )

    raw[1].wait_recv()
    raw[2].wait_recv()

    def dhid_arrive(origin, carry):
        pass_dhid(origin).wait_recv()
        return carry

    lax.fori_loop(0, fsdp, dhid_arrive, 0)

    def early_average(c, carry):
        at = rows_of(c - LATE)
        theirs = stepped(both(weight_theirs, at), both(dhid_theirs, at), tok_theirs[...])
        own[c] = averaged(own[c], theirs)
        for copy in results(c, own, rows_of(c)):
            copy.start()
        return carry

    lax.fori_loop(LATE, CHUNKS, early_average, 0)

    def late_average(c, carry):
        exchange(c).wait_recv()
        landed[c] = averaged(own[c], landed[c])
        for copy in results(c, landed, rows_of(c)):
            copy.start()
        return carry

    lax.fori_loop(0, LATE, late_average, 0)

    def finish(ref):
        def one(c, carry):
            for copy in results(c, ref, rows_of(c)):
                copy.wait()
            return carry

        return one

    def sent(c, carry):
        exchange(c).wait_send()
        return carry

    def dhid_sent(origin, carry):
        pass_dhid(origin).wait_send()
        return carry

    lax.fori_loop(0, LATE, sent, 0)
    lax.fori_loop(0, fsdp, dhid_sent, 0)
    for copy in raw:
        copy.wait_send()

    for a in range(3):
        for step in range(deep):
            left, right = me - 2 * step, me + 2 * step

            @pl.when(z - step >= 0)
            def _():
                @pl.when(has_next)
                def _():
                    hop(a, left, 0).wait_send()

                hop(a, left, 2).wait_send()

            @pl.when(z + step < deep)
            def _():
                @pl.when(has_prev)
                def _():
                    hop(a, right, 1).wait_send()

                if step > 0:
                    hop(a, right, 2).wait_send()

    lax.fori_loop(LATE, CHUNKS, finish(own), 0)
    lax.fori_loop(0, LATE, finish(landed), 0)


def solution(mesh):
    fsdp, peers = mesh.shape["fsdp"], mesh.shape["peer"]

    def body(tokens, gate_weight, up_weight, down_weight, cotangent):
        _, part, width = tokens.shape
        rows = gate_weight.shape[1]
        every = part * fsdp
        chunk = rows // CHUNKS
        bf16 = jnp.bfloat16
        result = jax.ShapeDtypeStruct((1, rows, width), bf16)
        flops = 10 * every * rows * width
        return pl.pallas_call(
            functools.partial(kernel, fsdp, peers),
            out_shape=(result, result),
            in_specs=[pl.BlockSpec(memory_space=pl.ANY)] * 5,
            out_specs=(pl.BlockSpec(memory_space=pl.ANY),) * 2,
            scratch_shapes=[
                pltpu.VMEM((every, width), bf16),
                pltpu.VMEM((every, width), bf16),
                pltpu.VMEM((rows, width), bf16),
                pltpu.VMEM((rows, width), bf16),
                pltpu.VMEM((rows, width), bf16),
                pltpu.VMEM((every, width), bf16),
                pltpu.VMEM((2, rows, every), bf16),
                pltpu.VMEM((2, EARLY * chunk, every), bf16),
                pltpu.VMEM((2, EARLY * chunk, width), bf16),
                pltpu.VMEM((CHUNKS, 2 * chunk, width), bf16),
                pltpu.VMEM((LATE, 2 * chunk, width), bf16),
                pltpu.SemaphoreType.DMA((5,)),
                pltpu.SemaphoreType.DMA((3, fsdp, 3)),
                pltpu.SemaphoreType.DMA((3, fsdp)),
                pltpu.SemaphoreType.DMA((LATE,)),
                pltpu.SemaphoreType.DMA((LATE,)),
                pltpu.SemaphoreType.DMA((3,)),
                pltpu.SemaphoreType.DMA((3,)),
                pltpu.SemaphoreType.DMA((fsdp,)),
                pltpu.SemaphoreType.DMA((fsdp,)),
                pltpu.SemaphoreType.DMA((2, CHUNKS)),
            ],
            compiler_params=pltpu.CompilerParams(
                collective_id=0, has_side_effects=True, vmem_limit_bytes=56 * 2**20
            ),
            cost_estimate=pl.CostEstimate(
                flops=flops, bytes_accessed=10 * rows * width, transcendentals=every * rows
            ),
        )(tokens, gate_weight, up_weight, down_weight, cotangent)

    spec = P("peer", "fsdp", None)
    return jax.shard_map(
        body, mesh=mesh, in_specs=(spec,) * 5, out_specs=(spec, spec), check_vma=False
    )
```

time: 232 us -> 179 us (0.77)
  Pallas kernels: 225 us -> 172 us
    pallas_call x1, Pallas kernels: 225 us -> 172 us  [body(): pl.pallas_call(functools.partial(kernel, fsdp, peers), out_shape=(result,...]
where the time goes in v2:
time: 179 us; the launch traced here: 178 us
  Pallas kernels  172 us (96%)
  local copies, waits for them, and re-layouts  5.5 us (3%)
    pallas_call x1, Pallas kernels, body(): pl.pallas_call(functools.partial(kernel, fsdp, peers), out_shape=(result,...  172 us
    unnamed x4, local copies, waits for them, and re-layouts  5.5 us

profile of v2, /device:TPU:0, one launch (start us, length us, event | category | flops | bytes accessed | tf_op | source)
XLA Modules:
  0.0 178.4 jit_solution(4235860375676253503)
XLA Ops:
  0.6 172.3 %shard_map.68 = (bf16[1,704,2048]{2,1,0:T(8,128)(2,1)}, bf16[1,704,2048]{2,1,0:T(8,128)(2,1)}) custom-call(bf16[1,128,2048]{2,1,0:T(8,128)(2,1)} %tok_in.1, bf16[1,704,2048]{2,1,0:T(8,128)(2,1)} %gate_in.1, bf16[1,704,2048]{2,1,0:T(8,128)(2,1)} %up_in.1, bf16[1,704,2048]{2,1,0:T(8,128)(2,1)} %down_in.1, bf16[1,128,2048]{2,1,0:T(8,128)(2,1)} %cot_in.1), custom_call_target="tpu_custom_call" | custom-call | flops 14763950080 | bytes 14417920 | tf_op jit(solution)/shard_map/pallas_call | solution.py:387
  172.9 0.0 copy-start
  172.9 3.9 %copy.9 = bf16[1,704,2048]{2,1,0:T(8,128)(2,1)} copy(bf16[1,704,2048]{2,1,0:T(8,128)(2,1)} %get-tuple-element.4) | data formatting | bytes 5767168
  176.8 0.0 copy-done
  176.8 1.6 copy.10
Async XLA Ops:
  172.9 3.9 %copy-start = (bf16[1,704,2048]{2,1,0:T(8,128)(2,1)S(1)}, bf16[1,704,2048]{2,1,0:T(8,128)(2,1)}, u32[]{:S(2)}) copy-start(bf16[1,704,2048]{2,1,0:T(8,128)(2,1)} %get-tuple-element.5) | copy-start | bytes 8650756

commit v3 on v2

--- a/solution.py
+++ b/solution.py
@@ -11,6 +11,7 @@
 CHUNKS = 11
 EARLY = 5
 LATE = CHUNKS - EARLY
+CROSS = 16
 RATE = 1.0
 MESH = pl.DeviceIdType.MESH
 
@@ -40,6 +41,8 @@
     dhid,
     dhid_theirs,
     weight_theirs,
+    gates,
+    uppers,
     own,
     landed,
     load_sem,
@@ -68,8 +71,14 @@
     from_peer = lax.rem(peer + peers - HOP, peers)
     has_prev, has_next = z > 0, z < deep - 1
 
-    ins = (tok_in, cot_in)
-    bufs = (tok, cot, tok_theirs)
+    straight = part - CROSS
+    pieces = (
+        (tok_in, tok, 0, straight),
+        (cot_in, cot, 0, straight),
+        (tok_in, tok_theirs, 0, part),
+        (tok_in, tok, straight, CROSS),
+        (cot_in, cot, straight, CROSS),
+    )
     early_rows = pl.ds(LATE * chunk, EARLY * chunk)
 
     loads = [
@@ -81,8 +90,8 @@
         return pl.ds(pl.multiple_of(origin * part, part), part)
 
     loads += [
-        pltpu.make_async_copy(ins[a].at[0], bufs[a].at[span(me), :], load_sem.at[3 + a])
-        for a in range(2)
+        pltpu.make_async_copy(source.at[0], target.at[span(me), :], load_sem.at[3 + a])
+        for a, (source, target) in enumerate(((tok_in, tok), (cot_in, cot)))
     ]
     for load in reversed(loads):
         load.start()
@@ -108,9 +117,10 @@
 
     def hop(a, origin, way, first=False):
         target = (me + 2, me - 2, across)[way]
-        here = bufs[a].at[span(origin), :]
+        source, buffer, start, size = pieces[a]
+        here = buffer.at[pl.ds(pl.multiple_of(origin * part + start, 16), size), :]
         return pltpu.make_async_remote_copy(
-            src_ref=ins[a].at[0] if first else here,
+            src_ref=source.at[0, pl.ds(start, size), :] if first else here,
             dst_ref=here,
             send_sem=send_sem.at[a, origin, way],
             recv_sem=recv_sem.at[a, origin],
@@ -121,19 +131,28 @@
     def arrive(a, origin):
         hop(a, origin, 2).wait_recv()
 
-    def first_hops(a, first):
+    def along(a, origin, first):
         @pl.when(has_next)
         def _():
-            hop(a, me, 0, first).start()
+            hop(a, origin, 0, first).start()
 
         @pl.when(has_prev)
         def _():
-            hop(a, me, 1, first).start()
-
+            hop(a, origin, 1, first).start()
+
+    def first_hops(a, first):
+        along(a, me, first)
         hop(a, me, 2, first).start()
 
-    for a in range(2):
+    for a in (3, 4):
+        hop(a, me, 2, True).start()
+    for a in (0, 1):
         first_hops(a, True)
+    for a in (3, 4):
+        along(a, me, True)
+    for a in (3, 4):
+        arrive(a, across)
+        along(a, across, False)
 
     def to_partner(source, target, sent, received):
         return pltpu.make_async_remote_copy(
@@ -166,14 +185,23 @@
             dhid_recv.at[origin],
         )
 
-    def forward(origin):
+    half = rows // 2
+
+    def half_at(i):
+        return pl.ds(pl.multiple_of(i * half, half), half)
+
+    def forward(origin, wait_tok, wait_cot):
         lanes = span(origin)
-        half = rows // 2
-
-        def some(i, carry):
-            at = pl.ds(pl.multiple_of(i * half, half), half)
-            gate = nt(wg[at, :], tok[lanes, :]) * in_scale
-            upper = nt(wu[at, :], tok[lanes, :]) * in_scale
+
+        def projections(i, carry):
+            at = half_at(i)
+            gates[at, :] = nt(wg[at, :], tok[lanes, :]) * in_scale
+            uppers[at, :] = nt(wu[at, :], tok[lanes, :]) * in_scale
+            return carry
+
+        def hidden(i, carry):
+            at = half_at(i)
+            gate, upper = gates[at, :], uppers[at, :]
             dhidden = nt(wd[at, :], cot[lanes, :]) * hidden_scale
             sigma = jax.nn.sigmoid(gate)
             dhid[0, at, lanes] = (
@@ -182,12 +210,18 @@
             dhid[1, at, lanes] = (dhidden * gate * sigma).astype(jnp.bfloat16)
             return carry
 
-        lax.fori_loop(0, 2, some, 0)
+        wait_tok()
+        lax.fori_loop(0, 2, projections, 0)
+        wait_cot()
+        lax.fori_loop(0, 2, hidden, 0)
         pass_dhid(origin).start()
+
+    def nothing():
+        pass
 
     for load in loads:
         load.wait()
-    forward(me)
+    forward(me, nothing, nothing)
 
     def relay(step, arrays):
         left, right = me - 2 * step, me + 2 * step
@@ -212,39 +246,62 @@
 
                 hop(a, right, 2).start()
 
-    def gather(step, arrays, use):
+    def relay_crossed(step):
         left, right = me - 2 * step, me + 2 * step
+        far_left, far_right = across - 2 * step, across + 2 * step
+
+        @pl.when(z - step >= 0)
+        def _():
+            for a, origin in ((3, left), (4, left), (3, far_left), (4, far_left)):
+                arrive(a, origin)
+
+                @pl.when(has_next)
+                def _():
+                    hop(a, origin, 0).start()
+
+        @pl.when(z + step < deep)
+        def _():
+            for a, origin in ((3, right), (4, right), (3, far_right), (4, far_right)):
+                arrive(a, origin)
+
+                @pl.when(has_prev)
+                def _():
+                    hop(a, origin, 1).start()
+
+    def near(step, use):
         near_left, near_right = across - 2 * (step - 1), across + 2 * (step - 1)
-        if step < deep:
-            relay(step, arrays)
-            if use is forward:
-                if step == deep - 1:
-                    raw[0].wait_recv()
-                    first_hops(2, False)
-
-                @pl.when(z - step >= 0)
-                def _():
-                    forward(left)
-
-                @pl.when(z + step < deep)
-                def _():
-                    forward(right)
 
         @pl.when(z - step + 1 >= 0)
         def _():
-            for a in arrays:
-                arrive(a, near_left)
             use(near_left)
 
         if step > 1:
             @pl.when(z + step - 1 < deep)
             def _():
-                for a in arrays:
-                    arrive(a, near_right)
                 use(near_right)
 
+    def forward_near(origin):
+        forward(
+            origin, functools.partial(arrive, 0, origin), functools.partial(arrive, 1, origin)
+        )
+
     for step in range(1, deep + 1):
-        gather(step, (0, 1), forward)
+        if step < deep:
+            relay(step, (0, 1))
+            relay_crossed(step)
+            if step == deep - 1:
+                raw[0].wait_recv()
+                first_hops(2, False)
+
+            @pl.when(z - step >= 0)
+            def _():
+                forward(me - 2 * step, nothing, nothing)
+
+            @pl.when(z + step < deep)
+            def _():
+                forward(me + 2 * step, nothing, nothing)
+
+        near(step, forward_near)
 
     def rows_of(c):
         return pl.ds(pl.multiple_of(c * chunk, chunk), chunk)
@@ -277,16 +334,15 @@
     def early(c, carry):
         step_own(c)
         return carry
-
-    def unused(origin):
-        pass
 
     begin = 0
     for step in range(1, deep + 1):
         end = -(-LATE * step // deep)
         lax.fori_loop(begin, end, late, 0)
         begin = end
-        gather(step, (2,), unused)
+        if step < deep:
+            relay(step, (2,))
+        near(step, functools.partial(arrive, 2))
     lax.fori_loop(LATE, CHUNKS, early, 0)
 
     def results(c, ref, at):
@@ -368,6 +424,19 @@
 
                 if step > 0:
                     hop(a, right, 2).wait_send()
+
+    for a in (3, 4):
+        hop(a, me, 2).wait_send()
+        for step in range(deep):
+            @pl.when(has_next & (z - step >= 0))
+            def _():
+                hop(a, me - 2 * step, 0).wait_send()
+                hop(a, across - 2 * step, 0).wait_send()
+
+            @pl.when(has_prev & (z + step < deep))
+            def _():
+                hop(a, me + 2 * step, 1).wait_send()
+                hop(a, across + 2 * step, 1).wait_send()
 
     lax.fori_loop(LATE, CHUNKS, finish(own), 0)
     lax.fori_loop(0, LATE, finish(landed), 0)
@@ -399,11 +468,13 @@
                 pltpu.VMEM((2, rows, every), bf16),
                 pltpu.VMEM((2, EARLY * chunk, every), bf16),
                 pltpu.VMEM((2, EARLY * chunk, width), bf16),
+                pltpu.VMEM((rows, part), jnp.float32),
+                pltpu.VMEM((rows, part), jnp.float32),
                 pltpu.VMEM((CHUNKS, 2 * chunk, width), bf16),
                 pltpu.VMEM((LATE, 2 * chunk, width), bf16),
                 pltpu.SemaphoreType.DMA((5,)),
-                pltpu.SemaphoreType.DMA((3, fsdp, 3)),
-                pltpu.SemaphoreType.DMA((3, fsdp)),
+                pltpu.SemaphoreType.DMA((5, fsdp, 3)),
+                pltpu.SemaphoreType.DMA((5, fsdp)),
                 pltpu.SemaphoreType.DMA((LATE,)),
                 pltpu.SemaphoreType.DMA((LATE,)),
                 pltpu.SemaphoreType.DMA((3,)),
@@ -413,7 +484,7 @@
                 pltpu.SemaphoreType.DMA((2, CHUNKS)),
             ],
             compiler_params=pltpu.CompilerParams(
-                collective_id=0, has_side_effects=True, vmem_limit_bytes=56 * 2**20
+                collective_id=0, has_side_effects=True, vmem_limit_bytes=46 * 2**20
             ),
             cost_estimate=pl.CostEstimate(
                 flops=flops, bytes_accessed=10 * rows * width, transcendentals=every * rows

time: 179 us -> 181 us (1.011)
  Pallas kernels: 172 us -> 175 us
    pallas_call x1, Pallas kernels: 172 us -> 175 us  [body(): pl.pallas_call(functools.partial(kernel, fsdp, peers), out_shape=(result,...]
    unnamed x4 -> x6, local copies, waits for them, and re-layouts: 5.5 us -> 5.23 us
where the time goes in v3:
time: 181 us; the launch traced here: 180 us
  Pallas kernels  175 us (97%)
  local copies, waits for them, and re-layouts  5.23 us (3%)
    pallas_call x1, Pallas kernels, body(): pl.pallas_call(functools.partial(kernel, fsdp, peers), out_shape=(result,...  175 us
    unnamed x6, local copies, waits for them, and re-layouts  5.23 us

profile of v3, /device:TPU:0, one launch (start us, length us, event | category | flops | bytes accessed | tf_op | source)
XLA Modules:
  0.0 180.4 jit_solution(17923009347853120065)
XLA Ops:
  0.6 0.0 copy-start
  0.6 1.0 copy-done
  1.7 0.0 copy-start.1
  1.7 1.0 copy-done.1
  2.7 174.5 %shard_map.68 = (bf16[1,704,2048]{2,1,0:T(8,128)(2,1)S(1)}, bf16[1,704,2048]{2,1,0:T(8,128)(2,1)S(1)}) custom-call(bf16[1,128,2048]{2,1,0:T(8,128)(2,1)S(1)} %copy-done, bf16[1,704,2048]{2,1,0:T(8,128)(2,1)} %gate_in.1, bf16[1,704,2048]{2,1,0:T(8,128)(2,1)} %up_in.1, bf16[1,704,2048]{2,1,0:T(8,128)(2,1)} %down_in.1, bf16[1,128,2048]{2,1,0:T(8,128)(2,1)S(1)} %copy-done.1), custom_call_target="tpu_custom_call" | custom-call | flops 14763950080 | bytes 14417920 | tf_op jit(solution)/shard_map/pallas_call | solution.py:456
  177.2 1.6 copy.9
  178.8 1.6 copy.10
Async XLA Ops:
  0.6 1.0 copy-start
  1.7 1.0 copy-start.1

commit v4 on v2

--- a/solution.py
+++ b/solution.py
@@ -11,6 +11,7 @@
 CHUNKS = 11
 EARLY = 5
 LATE = CHUNKS - EARLY
+COLUMNS = 512
 RATE = 1.0
 MESH = pl.DeviceIdType.MESH
 
@@ -40,6 +41,9 @@
     dhid,
     dhid_theirs,
     weight_theirs,
+    gates,
+    uppers,
+    settled,
     own,
     landed,
     load_sem,
@@ -68,8 +72,7 @@
     from_peer = lax.rem(peer + peers - HOP, peers)
     has_prev, has_next = z > 0, z < deep - 1
 
-    ins = (tok_in, cot_in)
-    bufs = (tok, cot, tok_theirs)
+    pieces = ((tok_in, tok), (cot_in, cot), (tok_in, tok_theirs))
     early_rows = pl.ds(LATE * chunk, EARLY * chunk)
 
     loads = [
@@ -81,8 +84,8 @@
         return pl.ds(pl.multiple_of(origin * part, part), part)
 
     loads += [
-        pltpu.make_async_copy(ins[a].at[0], bufs[a].at[span(me), :], load_sem.at[3 + a])
-        for a in range(2)
+        pltpu.make_async_copy(source.at[0], target.at[span(me), :], load_sem.at[3 + a])
+        for a, (source, target) in enumerate(((tok_in, tok), (cot_in, cot)))
     ]
     for load in reversed(loads):
         load.start()
@@ -108,9 +111,10 @@
 
     def hop(a, origin, way, first=False):
         target = (me + 2, me - 2, across)[way]
-        here = bufs[a].at[span(origin), :]
+        source, buffer = pieces[a]
+        here = buffer.at[span(origin), :]
         return pltpu.make_async_remote_copy(
-            src_ref=ins[a].at[0] if first else here,
+            src_ref=source.at[0] if first else here,
             dst_ref=here,
             send_sem=send_sem.at[a, origin, way],
             recv_sem=recv_sem.at[a, origin],
@@ -132,7 +136,7 @@
 
         hop(a, me, 2, first).start()
 
-    for a in range(2):
+    for a in (0, 1):
         first_hops(a, True)
 
     def to_partner(source, target, sent, received):
@@ -158,22 +162,35 @@
     for copy in raw:
         copy.start()
 
-    def pass_dhid(origin):
+    def pair(layer):
+        return pl.ds(pl.multiple_of(layer * 2 * part, 2 * part), 2 * part)
+
+    def pass_dhid(layer):
         return to_partner(
-            dhid.at[:, early_rows, span(origin)],
-            dhid_theirs.at[:, :, span(origin)],
-            dhid_send.at[origin],
-            dhid_recv.at[origin],
+            dhid.at[:, early_rows, pair(layer)],
+            dhid_theirs.at[:, :, pair(layer)],
+            dhid_send.at[layer],
+            dhid_recv.at[layer],
         )
 
-    def forward(origin):
-        lanes = span(origin)
-        half = rows // 2
-
-        def some(i, carry):
-            at = pl.ds(pl.multiple_of(i * half, half), half)
-            gate = nt(wg[at, :], tok[lanes, :]) * in_scale
-            upper = nt(wu[at, :], tok[lanes, :]) * in_scale
+    half = rows // 2
+
+    def half_at(i):
+        return pl.ds(pl.multiple_of(i * half, half), half)
+
+    def forward(layer):
+        lanes = pair(layer)
+        other = layer * 2 + 1 - y
+
+        def projections(i, carry):
+            at = half_at(i)
+            gates[at, :] = nt(wg[at, :], tok[lanes, :]) * in_scale
+            uppers[at, :] = nt(wu[at, :], tok[lanes, :]) * in_scale
+            return carry
+
+        def hidden(i, carry):
+            at = half_at(i)
+            gate, upper = gates[at, :], uppers[at, :]
             dhidden = nt(wd[at, :], cot[lanes, :]) * hidden_scale
             sigma = jax.nn.sigmoid(gate)
             dhid[0, at, lanes] = (
@@ -182,12 +199,14 @@
             dhid[1, at, lanes] = (dhidden * gate * sigma).astype(jnp.bfloat16)
             return carry
 
-        lax.fori_loop(0, 2, some, 0)
-        pass_dhid(origin).start()
+        arrive(0, other)
+        lax.fori_loop(0, 2, projections, 0)
+        arrive(1, other)
+        lax.fori_loop(0, 2, hidden, 0)
+        pass_dhid(layer).start()
 
     for load in loads:
         load.wait()
-    forward(me)
 
     def relay(step, arrays):
         left, right = me - 2 * step, me + 2 * step
@@ -212,48 +231,29 @@
 
                 hop(a, right, 2).start()
 
-    def gather(step, arrays, use):
-        left, right = me - 2 * step, me + 2 * step
-        near_left, near_right = across - 2 * (step - 1), across + 2 * (step - 1)
-        if step < deep:
-            relay(step, arrays)
-            if use is forward:
-                if step == deep - 1:
-                    raw[0].wait_recv()
-                    first_hops(2, False)
-
-                @pl.when(z - step >= 0)
-                def _():
-                    forward(left)
-
-                @pl.when(z + step < deep)
-                def _():
-                    forward(right)
-
+    def near(step, use):
         @pl.when(z - step + 1 >= 0)
         def _():
-            for a in arrays:
-                arrive(a, near_left)
-            use(near_left)
+            use(z - step + 1)
 
         if step > 1:
             @pl.when(z + step - 1 < deep)
             def _():
-                for a in arrays:
-                    arrive(a, near_right)
-                use(near_right)
+                use(z + step - 1)
 
     for step in range(1, deep + 1):
-        gather(step, (0, 1), forward)
+        if step < deep:
+            relay(step, (0, 1))
+            if step == deep - 1:
+                raw[0].wait_recv()
+                first_hops(2, False)
+        near(step, forward)
 
     def rows_of(c):
         return pl.ds(pl.multiple_of(c * chunk, chunk), chunk)
 
     def exchange(c):
         return to_partner(own.at[c], landed.at[c], peer_send.at[c], peer_recv.at[c])
-
-    def both(ref, at):
-        return jnp.concatenate([ref[0, at, :], ref[1, at, :]], axis=0)
 
     def stepped(weight, terms, tokens):
         grad = jnp.dot(terms, tokens, preferred_element_type=jnp.float32) * in_scale
@@ -267,84 +267,95 @@
     def step_own(c):
         at = rows_of(c)
         weight = jnp.concatenate([wg[at, :], wu[at, :]], axis=0)
-        own[c] = stepped(weight, both(dhid, at), tok[...])
+        terms = jnp.concatenate([dhid[0, at, :], dhid[1, at, :]], axis=0)
+        own[c] = stepped(weight, terms, tok[...])
 
     def late(c, carry):
         step_own(c)
         exchange(c).start()
         return carry
 
-    def early(c, carry):
-        step_own(c)
-        return carry
-
-    def unused(origin):
-        pass
+    def columns(i):
+        return pl.ds(pl.multiple_of(i * COLUMNS, COLUMNS), COLUMNS)
+
+    def early(i, carry):
+        cols = columns(i)
+        for k, weight in enumerate((wg, wu)):
+            settled[k, :, cols] = stepped(
+                weight[early_rows, cols], dhid[k, early_rows, :], tok[:, cols]
+            )
+        return carry
 
     begin = 0
     for step in range(1, deep + 1):
         end = -(-LATE * step // deep)
         lax.fori_loop(begin, end, late, 0)
         begin = end
-        gather(step, (2,), unused)
-    lax.fori_loop(LATE, CHUNKS, early, 0)
-
-    def results(c, ref, at):
+        if step < deep:
+            relay(step, (2,))
+        near(step, lambda layer: arrive(2, layer * 2 + 1 - y))
+    lax.fori_loop(0, width // COLUMNS, early, 0)
+
+    def results(c):
+        at = rows_of(c)
         return (
             pltpu.make_async_copy(
-                ref.at[c, pl.ds(0, chunk), :], gate_out.at[0, at, :], out_sem.at[0, c]
+                landed.at[c, pl.ds(0, chunk), :], gate_out.at[0, at, :], out_sem.at[0, c]
             ),
             pltpu.make_async_copy(
-                ref.at[c, pl.ds(chunk, chunk), :], up_out.at[0, at, :], out_sem.at[1, c]
+                landed.at[c, pl.ds(chunk, chunk), :], up_out.at[0, at, :], out_sem.at[1, c]
             ),
         )
 
+    early_results = [
+        pltpu.make_async_copy(settled.at[k], out.at[0, early_rows, :], out_sem.at[k, LATE])
+        for k, out in enumerate((gate_out, up_out))
+    ]
+
     raw[1].wait_recv()
     raw[2].wait_recv()
 
-    def dhid_arrive(origin, carry):
-        pass_dhid(origin).wait_recv()
-        return carry
-
-    lax.fori_loop(0, fsdp, dhid_arrive, 0)
-
-    def early_average(c, carry):
-        at = rows_of(c - LATE)
-        theirs = stepped(both(weight_theirs, at), both(dhid_theirs, at), tok_theirs[...])
-        own[c] = averaged(own[c], theirs)
-        for copy in results(c, own, rows_of(c)):
-            copy.start()
-        return carry
-
-    lax.fori_loop(LATE, CHUNKS, early_average, 0)
+    def dhid_arrive(layer, carry):
+        pass_dhid(layer).wait_recv()
+        return carry
+
+    lax.fori_loop(0, deep, dhid_arrive, 0)
+
+    def early_average(i, carry):
+        cols = columns(i)
+        for k in range(2):
+            theirs = stepped(weight_theirs[k, :, cols], dhid_theirs[k], tok_theirs[:, cols])
+            settled[k, :, cols] = averaged(settled[k, :, cols], theirs)
+        return carry
+
+    lax.fori_loop(0, width // COLUMNS, early_average, 0)
+    for copy in early_results:
+        copy.start()
 
     def late_average(c, carry):
         exchange(c).wait_recv()
         landed[c] = averaged(own[c], landed[c])
-        for copy in results(c, landed, rows_of(c)):
+        for copy in results(c):
             copy.start()
         return carry
 
     lax.fori_loop(0, LATE, late_average, 0)
 
-    def finish(ref):
-        def one(c, carry):
-            for copy in results(c, ref, rows_of(c)):
-                copy.wait()
-            return carry
-
-        return one
+    def finish(c, carry):
+        for copy in results(c):
+            copy.wait()
+        return carry
 
     def sent(c, carry):
         exchange(c).wait_send()
         return carry
 
-    def dhid_sent(origin, carry):
-        pass_dhid(origin).wait_send()
+    def dhid_sent(layer, carry):
+        pass_dhid(layer).wait_send()
         return carry
 
     lax.fori_loop(0, LATE, sent, 0)
-    lax.fori_loop(0, fsdp, dhid_sent, 0)
+    lax.fori_loop(0, deep, dhid_sent, 0)
     for copy in raw:
         copy.wait_send()
 
@@ -369,8 +380,9 @@
                 if step > 0:
                     hop(a, right, 2).wait_send()
 
-    lax.fori_loop(LATE, CHUNKS, finish(own), 0)
-    lax.fori_loop(0, LATE, finish(landed), 0)
+    for copy in early_results:
+        copy.wait()
+    lax.fori_loop(0, LATE, finish, 0)
 
 
 def solution(mesh):
@@ -387,7 +399,7 @@
         return pl.pallas_call(
             functools.partial(kernel, fsdp, peers),
             out_shape=(result, result),
-            in_specs=[pl.BlockSpec(memory_space=pl.ANY)] * 5,
+            in_specs=[pl.BlockSpec(memory_space=pltpu.HBM)] * 5,
             out_specs=(pl.BlockSpec(memory_space=pl.ANY),) * 2,
             scratch_shapes=[
                 pltpu.VMEM((every, width), bf16),
@@ -399,7 +411,10 @@
                 pltpu.VMEM((2, rows, every), bf16),
                 pltpu.VMEM((2, EARLY * chunk, every), bf16),
                 pltpu.VMEM((2, EARLY * chunk, width), bf16),
-                pltpu.VMEM((CHUNKS, 2 * chunk, width), bf16),
+                pltpu.VMEM((rows, 2 * part), jnp.float32),
+                pltpu.VMEM((rows, 2 * part), jnp.float32),
+                pltpu.VMEM((2, EARLY * chunk, width), bf16),
+                pltpu.VMEM((LATE, 2 * chunk, width), bf16),
                 pltpu.VMEM((LATE, 2 * chunk, width), bf16),
                 pltpu.SemaphoreType.DMA((5,)),
                 pltpu.SemaphoreType.DMA((3, fsdp, 3)),
@@ -408,12 +423,12 @@
                 pltpu.SemaphoreType.DMA((LATE,)),
                 pltpu.SemaphoreType.DMA((3,)),
                 pltpu.SemaphoreType.DMA((3,)),
-                pltpu.SemaphoreType.DMA((fsdp,)),
-                pltpu.SemaphoreType.DMA((fsdp,)),
-                pltpu.SemaphoreType.DMA((2, CHUNKS)),
+                pltpu.SemaphoreType.DMA((fsdp // 2,)),
+                pltpu.SemaphoreType.DMA((fsdp // 2,)),
+                pltpu.SemaphoreType.DMA((2, LATE + 1)),
             ],
             compiler_params=pltpu.CompilerParams(
-                collective_id=0, has_side_effects=True, vmem_limit_bytes=56 * 2**20
+                collective_id=0, has_side_effects=True, vmem_limit_bytes=46 * 2**20
             ),
             cost_estimate=pl.CostEstimate(
                 flops=flops, bytes_accessed=10 * rows * width, transcendentals=every * rows

time: 179 us -> 180 us (level)
  Pallas kernels: 172 us -> 174 us
    unnamed x4 -> x6, local copies, waits for them, and re-layouts: 5.5 us -> 5.23 us
where the time goes in v4:
time: 180 us; the launch traced here: 179 us
  Pallas kernels  174 us (97%)
  local copies, waits for them, and re-layouts  5.23 us (3%)
    pallas_call x1, Pallas kernels, body(): pl.pallas_call(functools.partial(kernel, fsdp, peers), out_shape=(result,...  174 us
    unnamed x6, local copies, waits for them, and re-layouts  5.23 us

profile of v4, /device:TPU:0, one launch (start us, length us, event | category | flops | bytes accessed | tf_op | source)
XLA Modules:
  0.0 179.4 jit_solution(15960357349559102988)
XLA Ops:
  0.6 0.0 copy-start
  0.6 1.0 copy-done
  1.7 0.0 copy-start.1
  1.7 1.0 copy-done.1
  2.7 173.5 %shard_map.68 = (bf16[1,704,2048]{2,1,0:T(8,128)(2,1)S(1)}, bf16[1,704,2048]{2,1,0:T(8,128)(2,1)S(1)}) custom-call(bf16[1,128,2048]{2,1,0:T(8,128)(2,1)S(1)} %copy-done, bf16[1,704,2048]{2,1,0:T(8,128)(2,1)} %gate_in.1, bf16[1,704,2048]{2,1,0:T(8,128)(2,1)} %up_in.1, bf16[1,704,2048]{2,1,0:T(8,128)(2,1)} %down_in.1, bf16[1,128,2048]{2,1,0:T(8,128)(2,1)S(1)} %copy-done.1), custom_call_target="tpu_custom_call" | custom-call | flops 14763950080 | bytes 14417920 | tf_op jit(solution)/shard_map/pallas_call | solution.py:399
  176.3 1.6 copy.9
  177.8 1.6 copy.10
Async XLA Ops:
  0.6 1.0 copy-start
  1.7 1.0 copy-start.1

commit v5 on v4

--- a/solution.py
+++ b/solution.py
@@ -9,7 +9,7 @@
 
 HOP = 2
 CHUNKS = 11
-EARLY = 5
+EARLY = 6
 LATE = CHUNKS - EARLY
 COLUMNS = 512
 RATE = 1.0

time: 180 us -> 181 us (level)
  no operation moved by 1% of the time
where the time goes in v5:
time: 181 us
  Pallas kernels  175 us (97%)
  local copies, waits for them, and re-layouts  5.23 us (3%)
    pallas_call x1, Pallas kernels, body(): pl.pallas_call(functools.partial(kernel, fsdp, peers), out_shape=(result,...  175 us
    unnamed x6, local copies, waits for them, and re-layouts  5.23 us

profile of v5, /device:TPU:0, one launch (start us, length us, event | category | flops | bytes accessed | tf_op | source)
XLA Modules:
  0.0 181.0 jit_solution(11053088432821439632)
XLA Ops:
  0.6 0.0 copy-start
  0.6 1.0 copy-done
  1.7 0.0 copy-start.1
  1.7 1.0 copy-done.1
  2.7 175.1 %shard_map.68 = (bf16[1,704,2048]{2,1,0:T(8,128)(2,1)S(1)}, bf16[1,704,2048]{2,1,0:T(8,128)(2,1)S(1)}) custom-call(bf16[1,128,2048]{2,1,0:T(8,128)(2,1)S(1)} %copy-done, bf16[1,704,2048]{2,1,0:T(8,128)(2,1)} %gate_in.1, bf16[1,704,2048]{2,1,0:T(8,128)(2,1)} %up_in.1, bf16[1,704,2048]{2,1,0:T(8,128)(2,1)} %down_in.1, bf16[1,128,2048]{2,1,0:T(8,128)(2,1)S(1)} %copy-done.1), custom_call_target="tpu_custom_call" | custom-call | flops 14763950080 | bytes 14417920 | tf_op jit(solution)/shard_map/pallas_call | solution.py:399
  177.9 1.6 copy.9
  179.4 1.6 copy.10
Async XLA Ops:
  0.6 1.0 copy-start
  1.7 1.0 copy-start.1
